TPU v7x, 1024 devices: a whole 8x8x8 slice. The times are simulated.
1024 devices in a mesh: dp: 4 (over y_lo, core), blk: 32 (over y_hi, z), hid: 8 (over x).
Axes of the slice: x: 8, y: 8 (y_hi: 4, y_lo: 2; y = y_hi * 2 + y_lo), z: 8, core: 2. Of those that a mesh axis runs over, the one named last changes fastest.
Arguments:
- tokens: bfloat16 [1024, 4096], P('dp', 'blk'), may hold values from -6 to 6
- cotangent: bfloat16 [1024, 4096], P('dp', 'blk'), may hold values from -2 to 2
- gate_weight: bfloat16 [14336, 4096], P('hid', 'blk'), may hold values from -0.09375 to 0.09375
- up_weight: bfloat16 [14336, 4096], P('hid', 'blk'), may hold values from -0.09375 to 0.09375
- down_weight: bfloat16 [14336, 4096], P('hid', 'blk'), may hold values from -0.046875 to 0.046875
Outputs:
- input_grad: float32 [1024, 4096], P(('dp', 'hid'), 'blk')
- gate_grad: float32 [14336, 4096], P('hid', ('blk', 'dp'))
- up_grad: float32 [14336, 4096], P('hid', ('blk', 'dp'))
- down_grad: float32 [14336, 4096], P('hid', ('blk', 'dp'))
All inputs are finite; a program needn't handle non-finite values.
Results may differ from a plain program's by a relative error of at most 0.0029.
Values may be sent and summed in bfloat16 or wider, within the bound.
A program may use at most 32 MiB of HBM per device.

v0:
```python
import jax
import jax.numpy as jnp
from jax import lax
from jax.sharding import PartitionSpec as P

contract_last = (((1,), (1,)), ((), ()))
contract_first = (((0,), (0,)), ((), ()))


def local(tokens, cotangent, gate_weight, up_weight, down_weight):
    units = gate_weight.shape[0]

    def project(block, weight):
        return lax.dot_general(block, weight, contract_last, preferred_element_type=jnp.float32)

    joined = lax.psum_scatter(
        jnp.concatenate(
            [
                project(tokens, gate_weight),
                project(tokens, up_weight),
                project(cotangent, down_weight),
            ],
            axis=1,
        ),
        "blk",
        scatter_dimension=0,
        tiled=True,
    )
    gate_pre = joined[:, :units]
    up_pre = joined[:, units : 2 * units]
    grad_hidden = joined[:, 2 * units :]
    sigmoid_gate = jax.nn.sigmoid(gate_pre)
    silu_gate = gate_pre * sigmoid_gate
    hidden = (silu_gate * up_pre).astype(jnp.bfloat16)
    grad_up = (grad_hidden * silu_gate).astype(jnp.bfloat16)
    grad_gate = (
        grad_hidden * up_pre * sigmoid_gate * (1.0 + gate_pre * (1.0 - sigmoid_gate))
    ).astype(jnp.bfloat16)
    gate_rows, up_rows, hidden_rows = (
        lax.all_gather(grad_gate, "blk", axis=0, tiled=True),
        lax.all_gather(grad_up, "blk", axis=0, tiled=True),
        lax.all_gather(hidden, "blk", axis=0, tiled=True),
    )
    gate_acc = lax.dot_general(
        gate_rows, tokens, contract_first, preferred_element_type=jnp.float32
    )
    up_acc = lax.dot_general(up_rows, tokens, contract_first, preferred_element_type=jnp.float32)
    down_acc = lax.dot_general(
        hidden_rows, cotangent, contract_first, preferred_element_type=jnp.float32
    )
    result = jnp.dot(gate_rows, gate_weight, preferred_element_type=jnp.float32)
    input_grad = lax.psum_scatter(
        result + jnp.dot(up_rows, up_weight, preferred_element_type=jnp.float32),
        "hid",
        scatter_dimension=0,
        tiled=True,
    )
    gate_grad, up_grad, down_grad = (
        lax.psum_scatter(gate_acc, "dp", scatter_dimension=1, tiled=True),
        lax.psum_scatter(up_acc, "dp", scatter_dimension=1, tiled=True),
        lax.psum_scatter(down_acc, "dp", scatter_dimension=1, tiled=True),
    )
    return (input_grad, gate_grad, up_grad, down_grad)


def solution(mesh):
    return jax.shard_map(
        local,
        mesh=mesh,
        in_specs=(
            P("dp", "blk"),
            P("dp", "blk"),
            P("hid", "blk"),
            P("hid", "blk"),
            P("hid", "blk"),
        ),
        out_specs=(
            P(("dp", "hid"), "blk"),
            P("hid", ("blk", "dp")),
            P("hid", ("blk", "dp")),
            P("hid", ("blk", "dp")),
        ),
        check_vma=False,
    )
```

profile of v0, /device:TPU:1, one launch (start us, length us, event | category | flops | bytes accessed | tf_op | source)
XLA Modules:
  0.0 665.1 jit_solution(14206267468081319112)
XLA Ops:
  7.2 0.0 reduce-scatter.6.cloned.1.call-start
  7.3 0.9 copy-done
  8.2 1.2 fusion.1
  9.4 0.4 fusion.2
  9.9 0.4 fusion.3
  10.3 2.8 pad_maximum_fusion
  13.0 0.0 reduce-scatter.8.cloned.1.call-start
  13.1 253.9 %reduce-scatter.6.cloned.1.call-done = f32[8,5376]{1,0:T(8,128)} async-done(((f32[256,5376]{1,0:T(8,128)}), f32[8,5376]{1,0:T(8,128)}) %reduce-scatter.6.cloned.1.call-update) | async-done | bytes 172048 | tf_op jit(solution)/shard_map/reduce_scatter | solution.py:16
  267.0 0.9 multiply_convert_fusion
  267.9 72.9 %all_gather.11 = bf16[256,1792]{1,0:T(8,128)(2,1)S(1)} all-gather(bf16[8,1792]{1,0:T(8,128)(2,1)S(1)} %get-tuple-element.4), channel_id=1, replica_groups=mesh['dp'=4,'blk'=32,'hid'=8] {'blk'}, dimensions={0}, use_global_device_ids=true | all-gather | bytes 946176 | tf_op jit(solution)/shard_map/all_gather | solution.py:42
  340.8 69.3 %all_gather.9 = bf16[256,1792]{1,0:T(8,128)(2,1)S(1)} all-gather(bf16[8,1792]{1,0:T(8,128)(2,1)S(1)} %get-tuple-element.5), channel_id=1, replica_groups=mesh['dp'=4,'blk'=32,'hid'=8] {'blk'}, dimensions={0}, use_global_device_ids=true | all-gather | bytes 946176 | tf_op jit(solution)/shard_map/all_gather | solution.py:40
  410.1 0.4 fusion.4
  410.5 69.5 %all_gather.10 = bf16[256,1792]{1,0:T(8,128)(2,1)S(1)} all-gather(bf16[8,1792]{1,0:T(8,128)(2,1)S(1)} %get-tuple-element.6), channel_id=1, replica_groups=mesh['dp'=4,'blk'=32,'hid'=8] {'blk'}, dimensions={0}, use_global_device_ids=true | all-gather | bytes 946176 | tf_op jit(solution)/shard_map/all_gather | solution.py:41
  479.9 1.0 convolution_add_fusion
  481.0 0.0 reduce-scatter.14.cloned.1.call-start
  481.1 1.3 fusion.7
  482.4 0.0 reduce-scatter.10.cloned.1.call-start
  482.4 1.3 fusion.5
  483.7 0.0 reduce-scatter.12.cloned.1.call-start
  483.8 1.3 fusion.6
  485.1 69.2 %reduce-scatter.8.cloned.1.call-done = f32[32,128]{1,0:T(8,128)} async-done(((f32[256,128]{1,0:T(8,128)}), f32[32,128]{1,0:T(8,128)}) %reduce-scatter.8.cloned.1.call-update) | async-done | bytes 16400 | tf_op jit(solution)/shard_map/reduce_scatter | solution.py:52
  554.3 38.3 %reduce-scatter.14.cloned.1.call-done = f32[1792,32]{0,1:T(8,128)} async-done(((f32[1792,128]{0,1:T(8,128)}), f32[1792,32]{0,1:T(8,128)}) %reduce-scatter.14.cloned.1.call-update) | async-done | bytes 229392 | tf_op jit(solution)/shard_map/reduce_scatter | solution.py:61
  592.6 33.0 %reduce-scatter.10.cloned.1.call-done = f32[1792,32]{0,1:T(8,128)} async-done(((f32[1792,128]{0,1:T(8,128)}), f32[1792,32]{0,1:T(8,128)}) %reduce-scatter.10.cloned.1.call-update) | async-done | bytes 229392 | tf_op jit(solution)/shard_map/reduce_scatter | solution.py:59
  625.6 33.0 %reduce-scatter.12.cloned.1.call-done = f32[1792,32]{0,1:T(8,128)} async-done(((f32[1792,128]{0,1:T(8,128)}), f32[1792,32]{0,1:T(8,128)}) %reduce-scatter.12.cloned.1.call-update) | async-done | bytes 229392 | tf_op jit(solution)/shard_map/reduce_scatter | solution.py:60
  (16 shorter events, 0.1 us)
Async XLA Ops:
  7.2 1.0 copy-start
  7.2 2.2 copy-start.3
  7.2 2.2 copy-start.1
  7.2 2.6 copy-start.5
  7.2 2.6 copy-start.4
  7.2 259.8 %reduce-scatter.6.cloned.1.call-start = ((), (), s32[]{:S(2)}) async-start(), calls=%async_computation.5 | async-start | bytes 5677056 | tf_op jit(solution)/shard_map/reduce_scatter | solution.py:16
  13.0 541.3 %reduce-scatter.8.cloned.1.call-start = ((), (), s32[]{:S(2)}) async-start(), calls=%async_computation.6 | async-start | bytes 147456 | tf_op jit(solution)/shard_map/reduce_scatter | solution.py:52
  340.8 139.1 %copy-start.2 = (bf16[1792,128]{1,0:T(8,128)(2,1)S(1)}, bf16[1792,128]{1,0:T(8,128)(2,1)}, u32[]{:S(2)}) copy-start(bf16[1792,128]{1,0:T(8,128)(2,1)} %param.8) | copy-start | bytes 1376260
  481.0 111.6 %reduce-scatter.14.cloned.1.call-start = ((), (), s32[]{:S(2)}) async-start(), calls=%async_computation.9 | async-start | bytes 1146880 | tf_op jit(solution)/shard_map/reduce_scatter | solution.py:61
  482.4 143.2 %reduce-scatter.10.cloned.1.call-start = ((), (), s32[]{:S(2)}) async-start(), calls=%async_computation.7 | async-start | bytes 1146880 | tf_op jit(solution)/shard_map/reduce_scatter | solution.py:59
  483.7 174.8 %reduce-scatter.12.cloned.1.call-start = ((), (), s32[]{:S(2)}) async-start(), calls=%async_computation.8 | async-start | bytes 1146880 | tf_op jit(solution)/shard_map/reduce_scatter | solution.py:60
Sparse Core Ops, SparseCore 0:
  13.8 253.2 reduce-scatter.5
  481.1 73.1 reduce-scatter.7
  558.7 33.8 reduce-scatter.13
  596.9 28.6 reduce-scatter.9
  629.8 28.6 reduce-scatter.11
where the time goes:
time: 665 us
  waiting for transfers between devices  427 us (64%)
  blocking collectives  212 us (32%)
  between operations  13.9 us (2%)
  matrix products  7.33 us (1%)
    reduce_scatter x1, waiting for transfers between devices, local(): lax.psum_scatter(jnp.concatenate([project(tokens, gate_weight), project(t...  254 us
    all_gather x1, blocking collectives, local(): lax.all_gather(hidden, 'blk', axis=0, tiled=True)  72.9 us
    all_gather x1, blocking collectives, local(): lax.all_gather(grad_up, 'blk', axis=0, tiled=True)  69.5 us
    all_gather x1, blocking collectives, local(): lax.all_gather(grad_gate, 'blk', axis=0, tiled=True)  69.3 us
    reduce_scatter x1, waiting for transfers between devices, local(): lax.psum_scatter(result + jnp.dot(up_rows, up_weight, preferred_element_t...  69.2 us
    reduce_scatter x1, waiting for transfers between devices, local(): lax.psum_scatter(down_acc, 'dp', scatter_dimension=1, tiled=True)  38.3 us
    reduce_scatter x1, waiting for transfers between devices, local(): lax.psum_scatter(gate_acc, 'dp', scatter_dimension=1, tiled=True)  33 us
    reduce_scatter x1, waiting for transfers between devices, local(): lax.psum_scatter(up_acc, 'dp', scatter_dimension=1, tiled=True)  33 us
  transfers between devices with their start and end apart: 5, of which 5 were waited for; matrix products, arithmetic and copies ran while one was open for 1% of the time, Pallas kernels for 0%

commit v1 on v0

v1 whole, which is shorter than its diff:
```python
import jax
import jax.numpy as jnp
from jax import lax
from jax.experimental import pallas as pl
from jax.experimental.pallas import tpu as pltpu
from jax.sharding import PartitionSpec as P

MESH = pl.DeviceIdType.MESH
NZ, NY, NX = 8, 4, 8
LANES = 128
CHUNKS = (128, 96)
F32, BF16 = jnp.float32, jnp.bfloat16
contract_last = (((1,), (1,)), ((), ()))
contract_first = (((0,), (0,)), ((), ()))
FAR_FIRST = (4, 3, 5, 2, 6, 1, 7)


def kernel(
    tok_in, cot_in, gate_w, up_w, down_w,
    ig_out, gate_out, up_out, down_out,
    tok, ig_send, ig_recv, ig_sum, ig_blocks,
    *rest,
):
    n_chunks = len(CHUNKS)
    names = ("g", "p", "rp", "h", "wg", "cr", "ls", "lr", "fs", "fr")
    bufs = []
    for k in range(n_chunks):
        bufs.append(dict(zip(names, rest[k * len(names):(k + 1) * len(names)])))
    (
        tz_s, tz_r, xr_s, xr_r, own_s,
        a_s, a_r, f_s, f_r, r_s, r_r, y_s, y_r, c_s, c_r, l_s, l_r, z_s, z_r,
        ix_s, ix_r, iz_s, iz_r,
    ) = rest[n_chunks * len(names):]

    dp = lax.axis_index("dp")
    blk = lax.axis_index("blk")
    x = lax.axis_index("hid")
    yh, z = blk // NZ, blk % NZ
    yl, c = dp // 2, dp % 2
    units = gate_w.shape[0] // NZ
    offs = [sum(CHUNKS[:k]) for k in range(n_chunks)]

    def at_z(v):
        return (dp, yh * NZ + v, x)

    def at_y(v):
        return (dp, v * NZ + z, x)

    def at_x(v):
        return (dp, blk, v)

    sibling = (yl * 2 + 1 - c, blk, x)
    across = ((1 - yl) * 2 + c, blk, x)

    def zj(j):
        return lax.rem(z + j, NZ)

    def yj(j):
        return lax.rem(yh + j, NY)

    def xj(j):
        return lax.rem(x + j, NX)

    barrier = pltpu.get_barrier_semaphore()
    peers = [at_z(zj(j)) for j in range(1, NZ)]
    peers += [at_x(xj(j)) for j in range(1, NX)]
    peers += [at_y(yj(j)) for j in range(1, NY)]
    peers += [sibling, across]
    for p in peers:
        pl.semaphore_signal(barrier, inc=1, device_id=p, device_id_type=MESH)
    pl.semaphore_wait(barrier, len(peers))

    pending = []

    def remote(src, dst, ss, rs, dev):
        return pltpu.make_async_remote_copy(
            src_ref=src, dst_ref=dst, send_sem=ss, recv_sem=rs,
            device_id=dev, device_id_type=MESH,
        )

    def go(copies):
        for cp in copies:
            cp.start()
        pending.extend(copies)
        return copies

    def arrived(copies):
        for cp in copies:
            cp.wait_recv()

    rows_x = tok_in.shape[0] // NX
    my_rows = pl.ds(pl.multiple_of(x * rows_x, rows_x), rows_x)
    my_lanes = pl.ds(pl.multiple_of(z * LANES, LANES), LANES)
    ins = (tok_in, cot_in)
    tz = go([
        remote(ins[a].at[my_rows, :], tok.at[a, my_rows, my_lanes], tz_s.at[a, j], tz_r.at[a, j], at_z(zj(j)))
        for j in FAR_FIRST for a in range(2)
    ])
    weights = (gate_w, up_w, down_w)

    def w_rows(k, to):
        nh = CHUNKS[k] // 2
        return pl.ds(pl.multiple_of(to * units + offs[k] + c * nh, 16), nh)

    def half(k, who):
        nh = CHUNKS[k] // 2
        return pl.ds(pl.multiple_of(who * nh, 16), nh)

    def push_weights(k):
        g = bufs[k]["g"]
        return go([
            remote(weights[m].at[w_rows(k, zj(j)), :], g.at[m, half(k, c), my_lanes], a_s.at[k, m, j], a_r.at[k, m, j], at_z(zj(j)))
            for j in FAR_FIRST for m in range(3)
        ])

    owns = []
    a_copies = [push_weights(0)]
    for a in range(2):
        owns.append(pltpu.make_async_copy(ins[a].at[my_rows, :], tok.at[a, my_rows, my_lanes], own_s.at[a]))
    for k in range(n_chunks):
        for m in range(3):
            owns.append(pltpu.make_async_copy(
                weights[m].at[w_rows(k, z), :], bufs[k]["g"].at[m, half(k, c), my_lanes], own_s.at[2 + k * 3 + m]))
    for cp in owns:
        cp.start()
    for k in range(1, n_chunks):
        a_copies.append(push_weights(k))
    for cp in owns:
        cp.wait()
    arrived(tz)

    def slice_at(d):
        return pl.ds(pl.multiple_of(lax.rem(x + d + NX, NX) * rows_x, rows_x), rows_x)

    for t in range(1, NX // 2 + 1):
        if t < NX // 2:
            right_ref, left_ref = tok.at[:, slice_at(1 - t), :], tok.at[:, slice_at(t - 1), :]
        else:
            right_ref, left_ref = tok.at[0, slice_at(1 - t), :], tok.at[1, slice_at(t - 1), :]
        step = go([
            remote(right_ref, right_ref, xr_s.at[0, t - 1], xr_r.at[0, t - 1], at_x(xj(1))),
            remote(left_ref, left_ref, xr_s.at[1, t - 1], xr_r.at[1, t - 1], at_x(xj(NX - 1))),
        ])
        if t == 1:
            arrived(a_copies[0])
            g0 = bufs[0]["g"].at[:, half(0, c), :]
            f_copies = [go([remote(g0, g0, f_s.at[0], f_r.at[0], sibling)])]
        arrived(step)

    def forward(k):
        arrived(a_copies[k])
        g = bufs[k]["g"].at[:, half(k, c), :]
        f_copies.append(go([remote(g, g, f_s.at[k], f_r.at[k], sibling)]))

    rows_y = tok_in.shape[0] // NY

    def project(k):
        arrived(f_copies[k])
        b = bufs[k]
        for m in range(3):
            part = lax.dot_general(tok[m // 2], b["g"][m], contract_last, preferred_element_type=F32)
            for q in range(NY):
                b["p"][q, m] = part[q * rows_y:(q + 1) * rows_y]
        return go([
            remote(b["p"].at[yj(j)], b["rp"].at[j - 1], r_s.at[k, j], r_r.at[k, j], at_y(yj(j)))
            for j in (2, 1, 3)
        ])

    def activate(k, copies):
        arrived(copies)
        b = bufs[k]
        gate_pre, up_pre, grad_hidden = [
            b["p"][yh, m] + b["rp"][0, m] + b["rp"][1, m] + b["rp"][2, m] for m in range(3)
        ]
        s = jax.nn.sigmoid(gate_pre)
        silu = gate_pre * s
        b["h"][yh, 0] = (grad_hidden * up_pre * s * (1.0 + gate_pre * (1.0 - s))).astype(BF16)
        b["h"][yh, 1] = (grad_hidden * silu).astype(BF16)
        b["h"][yh, 2] = (silu * up_pre).astype(BF16)
        mine = b["h"].at[yh]
        return go([
            remote(mine, mine, y_s.at[k, j], y_r.at[k, j], at_y(yj(j))) for j in (2, 1, 3)
        ])

    def backward(k, copies):
        arrived(copies)
        b = bufs[k]
        n = CHUNKS[k]
        grads = [
            jnp.concatenate([b["h"][q, m] for q in range(NY)], axis=0) for m in range(3)
        ]
        for m in range(3):
            full = lax.dot_general(tok[m // 2], grads[m], contract_first, preferred_element_type=F32)
            b["wg"][m] = full.reshape(NZ, 2, 2, LANES // 4, n)
        copies = go([remote(b["wg"].at[:, :, :, 1 - c], b["cr"], c_s.at[k], c_r.at[k], sibling)])
        part = jnp.dot(grads[0], b["g"][0], preferred_element_type=F32)
        part = part + jnp.dot(grads[1], b["g"][1], preferred_element_type=F32)
        return copies, part

    def over_y(k, copies):
        arrived(copies)
        b = bufs[k]
        b["ls"][...] = (b["wg"][:, :, 1 - yl, c] + b["cr"][:, :, 1 - yl]).astype(BF16)
        return go([remote(b["ls"], b["lr"], l_s.at[k], l_r.at[k], across)])

    def over_z(k, copies):
        arrived(copies)
        b = bufs[k]
        for m in range(3):
            done = b["wg"][m, :, yl, c] + b["cr"][m, :, yl] + b["lr"][m].astype(F32)
            b["fs"][:, m] = done.astype(BF16)
        b["fr"][z] = b["fs"][z]
        return go([
            remote(b["fs"].at[zj(j)], b["fr"].at[z], z_s.at[k, j], z_r.at[k, j], at_z(zj(j)))
            for j in FAR_FIRST
        ])

    outs = (gate_out, up_out, down_out)

    def finish(k, copies):
        arrived(copies)
        b = bufs[k]
        for q in range(NZ):
            for m in range(3):
                outs[m][q * units + offs[k]:q * units + offs[k] + CHUNKS[k], :] = b["fr"][q, m].astype(F32).T

    r0 = project(0)
    forward(1)
    y0 = activate(0, r0)
    r1 = project(1)
    c0, ig0 = backward(0, y0)
    ig_sum[...] = ig0
    y1 = activate(1, r1)
    l0 = over_y(0, c0)
    c1, ig1 = backward(1, y1)
    total = ig_sum[...] + ig1
    ig_sum[...] = total
    for q in range(NX):
        ig_send[q] = total[q * rows_x:(q + 1) * rows_x].astype(BF16)
    ix = go([
        remote(ig_send.at[xj(j)], ig_recv.at[j], ix_s.at[j], ix_r.at[j], at_x(xj(j))) for j in FAR_FIRST
    ])
    z0 = over_z(0, l0)
    l1 = over_y(1, c1)
    finish(0, z0)
    z1 = over_z(1, l1)
    arrived(ix)
    mine = ig_sum[my_rows, :]
    for j in range(1, NX):
        mine = mine + ig_recv[j].astype(F32)
    for q in range(NZ):
        ig_blocks[0, q] = mine[:, q * LANES:(q + 1) * LANES]
    iz = go([
        remote(ig_blocks.at[0, zj(j)], ig_blocks.at[1, j], iz_s.at[j], iz_r.at[j], at_z(zj(j))) for j in FAR_FIRST
    ])
    finish(1, z1)
    arrived(iz)
    result = ig_blocks[0, z]
    for j in range(1, NZ):
        result = result + ig_blocks[1, j]
    ig_out[...] = result
    for cp in pending:
        cp.wait_send()


def local(tokens, cotangent, gate_weight, up_weight, down_weight):
    rows, units_all = tokens.shape[0], gate_weight.shape[0]
    wide = NZ * LANES
    feats = LANES // 4
    scratch = [
        pltpu.VMEM((2, rows, wide), BF16),
        pltpu.VMEM((NX, rows // NX, wide), BF16),
        pltpu.VMEM((NX, rows // NX, wide), BF16),
        pltpu.VMEM((rows, wide), F32),
        pltpu.VMEM((2, NZ, rows // NX, LANES), F32),
    ]
    for n in CHUNKS:
        scratch += [
            pltpu.VMEM((3, n, wide), BF16),
            pltpu.VMEM((NY, 3, rows // NY, n), F32),
            pltpu.VMEM((NY - 1, 3, rows // NY, n), F32),
            pltpu.VMEM((NY, 3, rows // NY, n), BF16),
            pltpu.VMEM((3, NZ, 2, 2, feats, n), F32),
            pltpu.VMEM((3, NZ, 2, feats, n), F32),
            pltpu.VMEM((3, NZ, feats, n), BF16),
            pltpu.VMEM((3, NZ, feats, n), BF16),
            pltpu.VMEM((NZ, 3, feats, n), BF16),
            pltpu.VMEM((NZ, 3, feats, n), BF16),
        ]
    nc = len(CHUNKS)
    dma = pltpu.SemaphoreType.DMA
    scratch += [dma((2, NZ)), dma((2, NZ)), dma((2, NX // 2)), dma((2, NX // 2)), dma((2 + 3 * nc,))]
    for shape in ((nc, 3, NZ), (nc,), (nc, NY), (nc, NY), (nc,), (nc,), (nc, NZ), (NX,), (NZ,)):
        scratch += [dma(shape), dma(shape)]
    vmem = pl.BlockSpec(memory_space=pltpu.VMEM)
    grad = jax.ShapeDtypeStruct((units_all, feats), F32)
    return pl.pallas_call(
        kernel,
        out_shape=(jax.ShapeDtypeStruct((rows // NX, LANES), F32), grad, grad, grad),
        in_specs=[pl.BlockSpec(memory_space=pl.ANY)] * 5,
        out_specs=(vmem,) * 4,
        scratch_shapes=scratch,
        compiler_params=pltpu.CompilerParams(
            collective_id=0, has_side_effects=True, vmem_limit_bytes=48 * 2**20
        ),
    )(tokens, cotangent, gate_weight, up_weight, down_weight)


def solution(mesh):
    return jax.shard_map(
        local,
        mesh=mesh,
        in_specs=(
            P("dp", "blk"),
            P("dp", "blk"),
            P("hid", "blk"),
            P("hid", "blk"),
            P("hid", "blk"),
        ),
        out_specs=(
            P(("dp", "hid"), "blk"),
            P("hid", ("blk", "dp")),
            P("hid", ("blk", "dp")),
            P("hid", ("blk", "dp")),
        ),
        check_vma=False,
    )
```

time: 665 us -> 113 us (0.17)
  the two profiles are of different devices: /device:TPU:1 before, /device:TPU:17 now
where the time goes in v1:
time: 113 us; the launch traced here: 112 us
  Pallas kernels  104 us (92%)
  local copies, waits for them, and re-layouts  8.22 us (7%)
    pallas_call x1, Pallas kernels, local(): pl.pallas_call(kernel, out_shape=(jax.ShapeDtypeStruct((rows // NX, LANES...  104 us
    unnamed x11, local copies, waits for them, and re-layouts  5.33 us
    pallas_call x3, local copies, waits for them, and re-layouts, local(): pl.pallas_call(kernel, out_shape=(jax.ShapeDtypeStruct((rows // NX, LANES...  2.89 us

profile of v1, /device:TPU:17, one launch (start us, length us, event | category | flops | bytes accessed | tf_op | source)
XLA Modules:
  0.0 112.5 jit_solution(13170574921197651892)
XLA Ops:
  0.6 0.0 copy-start
  0.6 1.0 copy-done
  1.7 0.0 copy-start.1
  1.7 1.0 copy-done.1
  2.7 0.0 copy-start.2
  2.7 1.0 copy-done.2
  3.7 0.0 copy-start.3
  3.7 0.8 copy-done.3
  4.5 0.0 copy-start.4
  4.5 0.8 copy-done.4
  5.4 103.6 %shard_map.84 = (f32[32,128]{1,0:T(8,128)S(1)}, f32[1792,32]{1,0:T(8,128)S(1)}, f32[1792,32]{1,0:T(8,128)S(1)}, f32[1792,32]{1,0:T(8,128)S(1)}) custom-call(bf16[256,128]{1,0:T(8,128)(2,1)S(1)} %copy-done.3, bf16[256,128]{1,0:T(8,128)(2,1)S(1)} %copy-done.4, bf16[1792,128]{1,0:T(8,128)(2,1)S(1)} %copy-done, bf16[1792,128]{1,0:T(8,128)(2,1)S(1)} %copy-done.1, ...), custom_call_target="tpu_custom_call" | custom-call | tf_op jit(solution)/shard_map/pallas_call | solution.py:297
  109.0 1.0 copy.9
  110.0 1.0 copy.10
  110.9 1.0 copy.11
  111.9 0.6 copy.13
Async XLA Ops:
  0.6 1.0 copy-start
  1.7 1.0 copy-start.1
  2.7 1.0 copy-start.2
  3.7 0.8 copy-start.3
  4.5 0.8 copy-start.4

commit v2 on v1

--- a/solution.py
+++ b/solution.py
@@ -17,8 +17,8 @@
 
 def kernel(
     tok_in, cot_in, gate_w, up_w, down_w,
-    ig_out, gate_out, up_out, down_out,
-    tok, ig_send, ig_recv, ig_sum, ig_blocks,
+    ig_out, grad_out,
+    tok_own, w_own, tok, ig_send, ig_recv, ig_sum, ig_blocks,
     *rest,
 ):
     n_chunks = len(CHUNKS)
@@ -27,7 +27,7 @@
     for k in range(n_chunks):
         bufs.append(dict(zip(names, rest[k * len(names):(k + 1) * len(names)])))
     (
-        tz_s, tz_r, xr_s, xr_r, own_s,
+        in_s, tz_s, tz_r, xr_s, xr_r, own_s,
         a_s, a_r, f_s, f_r, r_s, r_r, y_s, y_r, c_s, c_r, l_s, l_r, z_s, z_r,
         ix_s, ix_r, iz_s, iz_r,
     ) = rest[n_chunks * len(names):]
@@ -37,8 +37,15 @@
     x = lax.axis_index("hid")
     yh, z = blk // NZ, blk % NZ
     yl, c = dp // 2, dp % 2
-    units = gate_w.shape[0] // NZ
-    offs = [sum(CHUNKS[:k]) for k in range(n_chunks)]
+    bases = [NZ * sum(CHUNKS[:k]) for k in range(n_chunks)]
+
+    loads = []
+    for i, ref in enumerate((tok_in, cot_in)):
+        loads.append(pltpu.make_async_copy(ref, tok_own.at[i], in_s.at[i]))
+    for i, ref in enumerate((gate_w, up_w, down_w)):
+        loads.append(pltpu.make_async_copy(ref, w_own.at[i], in_s.at[2 + i]))
+    for cp in loads:
+        cp.start()
 
     def at_z(v):
         return (dp, yh * NZ + v, x)
@@ -91,16 +98,16 @@
     rows_x = tok_in.shape[0] // NX
     my_rows = pl.ds(pl.multiple_of(x * rows_x, rows_x), rows_x)
     my_lanes = pl.ds(pl.multiple_of(z * LANES, LANES), LANES)
-    ins = (tok_in, cot_in)
+    loads[0].wait()
+    loads[1].wait()
     tz = go([
-        remote(ins[a].at[my_rows, :], tok.at[a, my_rows, my_lanes], tz_s.at[a, j], tz_r.at[a, j], at_z(zj(j)))
-        for j in FAR_FIRST for a in range(2)
+        remote(tok_own.at[:, my_rows, :], tok.at[:, my_rows, my_lanes], tz_s.at[j], tz_r.at[j], at_z(zj(j)))
+        for j in FAR_FIRST
     ])
-    weights = (gate_w, up_w, down_w)
 
     def w_rows(k, to):
         nh = CHUNKS[k] // 2
-        return pl.ds(pl.multiple_of(to * units + offs[k] + c * nh, 16), nh)
+        return pl.ds(pl.multiple_of(bases[k] + to * CHUNKS[k] + c * nh, 16), nh)
 
     def half(k, who):
         nh = CHUNKS[k] // 2
@@ -109,48 +116,55 @@
     def push_weights(k):
         g = bufs[k]["g"]
         return go([
-            remote(weights[m].at[w_rows(k, zj(j)), :], g.at[m, half(k, c), my_lanes], a_s.at[k, m, j], a_r.at[k, m, j], at_z(zj(j)))
-            for j in FAR_FIRST for m in range(3)
+            remote(w_own.at[:, w_rows(k, zj(j)), :], g.at[:, half(k, c), my_lanes], a_s.at[k, j], a_r.at[k, j], at_z(zj(j)))
+            for j in FAR_FIRST
         ])
 
-    owns = []
+    for cp in loads[2:]:
+        cp.wait()
     a_copies = [push_weights(0)]
-    for a in range(2):
-        owns.append(pltpu.make_async_copy(ins[a].at[my_rows, :], tok.at[a, my_rows, my_lanes], own_s.at[a]))
+    owns = [pltpu.make_async_copy(tok_own.at[:, my_rows, :], tok.at[:, my_rows, my_lanes], own_s.at[0])]
     for k in range(n_chunks):
-        for m in range(3):
-            owns.append(pltpu.make_async_copy(
-                weights[m].at[w_rows(k, z), :], bufs[k]["g"].at[m, half(k, c), my_lanes], own_s.at[2 + k * 3 + m]))
+        owns.append(pltpu.make_async_copy(
+            w_own.at[:, w_rows(k, z), :], bufs[k]["g"].at[:, half(k, c), my_lanes], own_s.at[1 + k]))
     for cp in owns:
         cp.start()
-    for k in range(1, n_chunks):
-        a_copies.append(push_weights(k))
     for cp in owns:
         cp.wait()
     arrived(tz)
 
-    def slice_at(d):
-        return pl.ds(pl.multiple_of(lax.rem(x + d + NX, NX) * rows_x, rows_x), rows_x)
-
-    for t in range(1, NX // 2 + 1):
-        if t < NX // 2:
-            right_ref, left_ref = tok.at[:, slice_at(1 - t), :], tok.at[:, slice_at(t - 1), :]
-        else:
-            right_ref, left_ref = tok.at[0, slice_at(1 - t), :], tok.at[1, slice_at(t - 1), :]
-        step = go([
-            remote(right_ref, right_ref, xr_s.at[0, t - 1], xr_r.at[0, t - 1], at_x(xj(1))),
-            remote(left_ref, left_ref, xr_s.at[1, t - 1], xr_r.at[1, t - 1], at_x(xj(NX - 1))),
-        ])
-        if t == 1:
-            arrived(a_copies[0])
-            g0 = bufs[0]["g"].at[:, half(0, c), :]
-            f_copies = [go([remote(g0, g0, f_s.at[0], f_r.at[0], sibling)])]
-        arrived(step)
+    f_copies = []
 
     def forward(k):
         arrived(a_copies[k])
         g = bufs[k]["g"].at[:, half(k, c), :]
         f_copies.append(go([remote(g, g, f_s.at[k], f_r.at[k], sibling)]))
+
+    part = rows_x // 2
+
+    def slice_at(d, i):
+        row = lax.rem(x + d + NX, NX) * rows_x + i % 2 * part
+        return i // 2, pl.ds(pl.multiple_of(row, part), part)
+
+    moving = {}
+    for t in range(1, NX // 2 + 1):
+        for i in range(4):
+            for way in range(2):
+                if t > 1:
+                    arrived(moving.pop((t - 1, i, way)))
+            for way in range(2):
+                if t == NX // 2 and i // 2 != way:
+                    continue
+                a, where = slice_at(1 - t if way == 0 else t - 1, i)
+                ref = tok.at[a, where, :]
+                moving[t, i, way] = go([
+                    remote(ref, ref, xr_s.at[way, t - 1, i], xr_r.at[way, t - 1, i], at_x(xj(1 if way == 0 else NX - 1)))
+                ])
+        if t == 3:
+            forward(0)
+            a_copies.append(push_weights(1))
+    for copies in moving.values():
+        arrived(copies)
 
     rows_y = tok_in.shape[0] // NY
 
@@ -215,19 +229,18 @@
             for j in FAR_FIRST
         ])
 
-    outs = (gate_out, up_out, down_out)
-
     def finish(k, copies):
         arrived(copies)
         b = bufs[k]
-        for q in range(NZ):
-            for m in range(3):
-                outs[m][q * units + offs[k]:q * units + offs[k] + CHUNKS[k], :] = b["fr"][q, m].astype(F32).T
+        n = CHUNKS[k]
+        for m in range(3):
+            row = jnp.concatenate([b["fr"][q, m] for q in range(NZ)], axis=1)
+            grad_out[m, :, bases[k]:bases[k] + NZ * n] = row
 
     r0 = project(0)
     forward(1)
+    r1 = project(1)
     y0 = activate(0, r0)
-    r1 = project(1)
     c0, ig0 = backward(0, y0)
     ig_sum[...] = ig0
     y1 = activate(1, r1)
@@ -263,11 +276,20 @@
         cp.wait_send()
 
 
+def widen(ig_in, grad_in, ig_out, gate_out, up_out, down_out):
+    ig_out[...] = ig_in[...]
+    gate_out[...] = grad_in[0].astype(F32)
+    up_out[...] = grad_in[1].astype(F32)
+    down_out[...] = grad_in[2].astype(F32)
+
+
 def local(tokens, cotangent, gate_weight, up_weight, down_weight):
     rows, units_all = tokens.shape[0], gate_weight.shape[0]
     wide = NZ * LANES
     feats = LANES // 4
     scratch = [
+        pltpu.VMEM((2, rows, LANES), BF16),
+        pltpu.VMEM((3, units_all, LANES), BF16),
         pltpu.VMEM((2, rows, wide), BF16),
         pltpu.VMEM((NX, rows // NX, wide), BF16),
         pltpu.VMEM((NX, rows // NX, wide), BF16),
@@ -289,21 +311,30 @@
         ]
     nc = len(CHUNKS)
     dma = pltpu.SemaphoreType.DMA
-    scratch += [dma((2, NZ)), dma((2, NZ)), dma((2, NX // 2)), dma((2, NX // 2)), dma((2 + 3 * nc,))]
-    for shape in ((nc, 3, NZ), (nc,), (nc, NY), (nc, NY), (nc,), (nc,), (nc, NZ), (NX,), (NZ,)):
+    scratch += [dma((5,)), dma((NZ,)), dma((NZ,)), dma((2, NX // 2, 4)), dma((2, NX // 2, 4)), dma((1 + nc,))]
+    for shape in ((nc, NZ), (nc,), (nc, NY), (nc, NY), (nc,), (nc,), (nc, NZ), (NX,), (NZ,)):
         scratch += [dma(shape), dma(shape)]
     vmem = pl.BlockSpec(memory_space=pltpu.VMEM)
-    grad = jax.ShapeDtypeStruct((units_all, feats), F32)
-    return pl.pallas_call(
+    hbm = pl.BlockSpec(memory_space=pltpu.HBM)
+    ig, grads = pl.pallas_call(
         kernel,
-        out_shape=(jax.ShapeDtypeStruct((rows // NX, LANES), F32), grad, grad, grad),
-        in_specs=[pl.BlockSpec(memory_space=pl.ANY)] * 5,
-        out_specs=(vmem,) * 4,
+        out_shape=(
+            jax.ShapeDtypeStruct((rows // NX, LANES), F32),
+            jax.ShapeDtypeStruct((3, feats, units_all), BF16),
+        ),
+        in_specs=[hbm] * 5,
+        out_specs=(vmem, vmem),
         scratch_shapes=scratch,
         compiler_params=pltpu.CompilerParams(
-            collective_id=0, has_side_effects=True, vmem_limit_bytes=48 * 2**20
+            collective_id=0, has_side_effects=True, vmem_limit_bytes=60 * 2**20
         ),
     )(tokens, cotangent, gate_weight, up_weight, down_weight)
+    grad = jax.ShapeDtypeStruct((feats, units_all), F32)
+    input_grad, *weight_grads = pl.pallas_call(
+        widen,
+        out_shape=(jax.ShapeDtypeStruct(ig.shape, F32), grad, grad, grad),
+    )(ig, grads)
+    return (input_grad, *[g.T for g in weight_grads])
 
 
 def solution(mesh):

time: 113 us -> 99.1 us (0.88)
  the two profiles are of different devices: /device:TPU:17 before, /device:TPU:1 now
where the time goes in v2:
time: 99.1 us; the launch traced here: 98.7 us
  Pallas kernels  98.1 us (99%)
    pallas_call x1, Pallas kernels, local(): pl.pallas_call(kernel, out_shape=(jax.ShapeDtypeStruct((rows // NX, LANES...  96.2 us

profile of v2, /device:TPU:1, one launch (start us, length us, event | category | flops | bytes accessed | tf_op | source)
XLA Modules:
  0.0 98.7 jit_solution(10859435314294970225)
XLA Ops:
  0.6 96.2 %shard_map.84 = (f32[32,128]{1,0:T(8,128)}, bf16[3,32,1792]{2,1,0:T(8,128)(2,1)}) custom-call(bf16[256,128]{1,0:T(8,128)(2,1)} %tok_in.1, bf16[256,128]{1,0:T(8,128)(2,1)} %cot_in.1, bf16[1792,128]{1,0:T(8,128)(2,1)} %gate_w.1, bf16[1792,128]{1,0:T(8,128)(2,1)} %up_w.1, bf16[1792,128]{1,0:T(8,128)(2,1)} %down_w.1), custom_call_target="tpu_custom_call" | custom-call | tf_op jit(solution)/shard_map/pallas_call | solution.py:319
  96.9 1.9 %shard_map.85 = (f32[32,128]{1,0:T(8,128)}, f32[32,1792]{1,0:T(8,128)}, f32[32,1792]{1,0:T(8,128)}, f32[32,1792]{1,0:T(8,128)}) custom-call(f32[32,128]{1,0:T(8,128)} %get-tuple-element.10.ig_in, bf16[3,32,1792]{2,1,0:T(8,128)(2,1)} %get-tuple-element.11.grad_in), custom_call_target="tpu_custom_call" | custom-call | tf_op jit(solution)/shard_map/pallas_call | solution.py:333

commit v3 on v2

--- a/solution.py
+++ b/solution.py
@@ -18,7 +18,7 @@
 def kernel(
     tok_in, cot_in, gate_w, up_w, down_w,
     ig_out, grad_out,
-    tok_own, w_own, tok, ig_send, ig_recv, ig_sum, ig_blocks,
+    tok_own, w_own, tok, ig_send, ig_recv, ig_send_z, ig_recv_z, ig_sum, ig_blocks, ig_blocks_x,
     *rest,
 ):
     n_chunks = len(CHUNKS)
@@ -29,7 +29,7 @@
     (
         in_s, tz_s, tz_r, xr_s, xr_r, own_s,
         a_s, a_r, f_s, f_r, r_s, r_r, y_s, y_r, c_s, c_r, l_s, l_r, z_s, z_r,
-        ix_s, ix_r, iz_s, iz_r,
+        ix_s, ix_r, iz_s, iz_r, bz_s, bz_r, bx_s, bx_r,
     ) = rest[n_chunks * len(names):]
 
     dp = lax.axis_index("dp")
@@ -122,7 +122,7 @@
 
     for cp in loads[2:]:
         cp.wait()
-    a_copies = [push_weights(0)]
+    a_copies = [push_weights(0), push_weights(1)]
     owns = [pltpu.make_async_copy(tok_own.at[:, my_rows, :], tok.at[:, my_rows, my_lanes], own_s.at[0])]
     for k in range(n_chunks):
         owns.append(pltpu.make_async_copy(
@@ -160,9 +160,8 @@
                 moving[t, i, way] = go([
                     remote(ref, ref, xr_s.at[way, t - 1, i], xr_r.at[way, t - 1, i], at_x(xj(1 if way == 0 else NX - 1)))
                 ])
-        if t == 3:
+        if t == NX // 2:
             forward(0)
-            a_copies.append(push_weights(1))
     for copies in moving.values():
         arrived(copies)
 
@@ -249,16 +248,22 @@
     total = ig_sum[...] + ig1
     ig_sum[...] = total
     for q in range(NX):
-        ig_send[q] = total[q * rows_x:(q + 1) * rows_x].astype(BF16)
+        rows_q = total[q * rows_x:(q + 1) * rows_x]
+        ig_send[q] = rows_q[:part].astype(BF16)
+        for w in range(NZ):
+            ig_send_z[w, q] = rows_q[part:, w * LANES:(w + 1) * LANES].astype(BF16)
     ix = go([
         remote(ig_send.at[xj(j)], ig_recv.at[j], ix_s.at[j], ix_r.at[j], at_x(xj(j))) for j in FAR_FIRST
+    ])
+    bz = go([
+        remote(ig_send_z.at[zj(j)], ig_recv_z.at[j], bz_s.at[j], bz_r.at[j], at_z(zj(j))) for j in FAR_FIRST
     ])
     z0 = over_z(0, l0)
     l1 = over_y(1, c1)
     finish(0, z0)
     z1 = over_z(1, l1)
     arrived(ix)
-    mine = ig_sum[my_rows, :]
+    mine = ig_sum[pl.ds(pl.multiple_of(x * rows_x, part), part), :]
     for j in range(1, NX):
         mine = mine + ig_recv[j].astype(F32)
     for q in range(NZ):
@@ -266,12 +271,22 @@
     iz = go([
         remote(ig_blocks.at[0, zj(j)], ig_blocks.at[1, j], iz_s.at[j], iz_r.at[j], at_z(zj(j))) for j in FAR_FIRST
     ])
+    arrived(bz)
+    for q in range(NX):
+        block = ig_sum[q * rows_x + part:(q + 1) * rows_x, my_lanes]
+        for j in range(1, NZ):
+            block = block + ig_recv_z[j, q].astype(F32)
+        ig_blocks_x[0, q] = block
+    bx = go([
+        remote(ig_blocks_x.at[0, xj(j)], ig_blocks_x.at[1, j], bx_s.at[j], bx_r.at[j], at_x(xj(j))) for j in FAR_FIRST
+    ])
     finish(1, z1)
-    arrived(iz)
-    result = ig_blocks[0, z]
-    for j in range(1, NZ):
-        result = result + ig_blocks[1, j]
-    ig_out[...] = result
+    for i, (copies, blocks, own) in enumerate(((iz, ig_blocks, z), (bx, ig_blocks_x, x))):
+        arrived(copies)
+        result = blocks[0, own]
+        for j in range(1, NZ):
+            result = result + blocks[1, j]
+        ig_out[i * part:(i + 1) * part, :] = result
     for cp in pending:
         cp.wait_send()
 
@@ -286,15 +301,19 @@
 def local(tokens, cotangent, gate_weight, up_weight, down_weight):
     rows, units_all = tokens.shape[0], gate_weight.shape[0]
     wide = NZ * LANES
+    part = rows // NX // 2
     feats = LANES // 4
     scratch = [
         pltpu.VMEM((2, rows, LANES), BF16),
         pltpu.VMEM((3, units_all, LANES), BF16),
         pltpu.VMEM((2, rows, wide), BF16),
-        pltpu.VMEM((NX, rows // NX, wide), BF16),
-        pltpu.VMEM((NX, rows // NX, wide), BF16),
+        pltpu.VMEM((NX, part, wide), BF16),
+        pltpu.VMEM((NX, part, wide), BF16),
+        pltpu.VMEM((NZ, NX, part, LANES), BF16),
+        pltpu.VMEM((NZ, NX, part, LANES), BF16),
         pltpu.VMEM((rows, wide), F32),
-        pltpu.VMEM((2, NZ, rows // NX, LANES), F32),
+        pltpu.VMEM((2, NZ, part, LANES), F32),
+        pltpu.VMEM((2, NX, part, LANES), F32),
     ]
     for n in CHUNKS:
         scratch += [
@@ -312,7 +331,7 @@
     nc = len(CHUNKS)
     dma = pltpu.SemaphoreType.DMA
     scratch += [dma((5,)), dma((NZ,)), dma((NZ,)), dma((2, NX // 2, 4)), dma((2, NX // 2, 4)), dma((1 + nc,))]
-    for shape in ((nc, NZ), (nc,), (nc, NY), (nc, NY), (nc,), (nc,), (nc, NZ), (NX,), (NZ,)):
+    for shape in ((nc, NZ), (nc,), (nc, NY), (nc, NY), (nc,), (nc,), (nc, NZ), (NX,), (NZ,), (NZ,), (NX,)):
         scratch += [dma(shape), dma(shape)]
     vmem = pl.BlockSpec(memory_space=pltpu.VMEM)
     hbm = pl.BlockSpec(memory_space=pltpu.HBM)

time: 99.1 us -> 102 us (1.029)
  the two profiles are of different devices: /device:TPU:1 before, /device:TPU:2 now
where the time goes in v3:
time: 102 us
  Pallas kernels  101 us (99%)
    pallas_call x1, Pallas kernels, local(): pl.pallas_call(kernel, out_shape=(jax.ShapeDtypeStruct((rows // NX, LANES...  99.2 us

profile of v3, /device:TPU:2, one launch (start us, length us, event | category | flops | bytes accessed | tf_op | source)
XLA Modules:
  0.0 101.7 jit_solution(12041320712933469832)
XLA Ops:
  0.6 99.2 %shard_map.84 = (f32[32,128]{1,0:T(8,128)}, bf16[3,32,1792]{2,1,0:T(8,128)(2,1)}) custom-call(bf16[256,128]{1,0:T(8,128)(2,1)} %tok_in.1, bf16[256,128]{1,0:T(8,128)(2,1)} %cot_in.1, bf16[1792,128]{1,0:T(8,128)(2,1)} %gate_w.1, bf16[1792,128]{1,0:T(8,128)(2,1)} %up_w.1, bf16[1792,128]{1,0:T(8,128)(2,1)} %down_w.1), custom_call_target="tpu_custom_call" | custom-call | tf_op jit(solution)/shard_map/pallas_call | solution.py:338
  99.8 1.9 %shard_map.85 = (f32[32,128]{1,0:T(8,128)}, f32[32,1792]{1,0:T(8,128)}, f32[32,1792]{1,0:T(8,128)}, f32[32,1792]{1,0:T(8,128)}) custom-call(f32[32,128]{1,0:T(8,128)} %get-tuple-element.10.ig_in, bf16[3,32,1792]{2,1,0:T(8,128)(2,1)} %get-tuple-element.11.grad_in), custom_call_target="tpu_custom_call" | custom-call | tf_op jit(solution)/shard_map/pallas_call | solution.py:352
